TPU v7x, 512 devices: a whole 4x8x8 slice. The times are simulated.
512 devices in a mesh: cp: 64 (over y_lo, z, x), dp: 8 (over y_hi, core).
Axes of the slice: x: 4, y: 8 (y_hi: 4, y_lo: 2; y = y_hi * 2 + y_lo), z: 8, core: 2. Of those that a mesh axis runs over, the one named last changes fastest.
Arguments:
- queries: bfloat16 [8, 8192, 512], P('dp', 'cp'), may hold values from -40 to 40
- keys: bfloat16 [8, 8192, 512], P('dp', 'cp'), may hold values from -4 to 4
- values: bfloat16 [8, 8192, 512], P('dp', 'cp'), may hold values from -6 to 6
- segments: int32 [8, 8192], P('dp'), may hold values from 0 to 127, never falling along the last dimension, each value on 1 to 384 neighbouring positions
- w_out: bfloat16 [512, 1024], replicated, may hold values from -0.25 to 0.25
- cotangent: bfloat16 [8, 8192, 1024], P('dp', 'cp'), may hold values from -16 to 16
Outputs:
- query_grad: float32 [8, 8192, 512], P('dp', 'cp')
- key_grad: float32 [8, 8192, 512], P('dp', 'cp')
- value_grad: float32 [8, 8192, 512], P('dp', 'cp')
- weight_grad: float32 [512, 1024], P('cp', 'dp')
Inputs may be any that keep to these rules, and one draw needn't show every extreme that they name: `segments`: in each stream the flow numbers never fall; each flow holds 1 to 384 consecutive positions and one holds exactly 384.
All inputs are finite; a program needn't handle non-finite values.
Results may differ from a plain program's by a relative error of at most 0.04.
Values may be sent and summed in bfloat16 or wider, within the bound.
A program may use at most 64 MiB of HBM per device.

v0:
```python
import math

import jax
import jax.numpy as jnp
from jax import lax
from jax.sharding import PartitionSpec as P

HEAD_DIM = 128
HOPS = 3


NEGATIVE = -1e30


def from_behind(value, axis, steps):
    count = lax.axis_size(axis)
    first, last = (max(0, -steps), min(count, count - steps))
    return lax.ppermute(value, axis, [(source, source + steps) for source in range(first, last)])


def log_total(scores):
    highest = jnp.max(scores, axis=-1, keepdims=True)
    summed = jnp.sum(jnp.exp(scores - highest), axis=-1, keepdims=True)
    return highest + jnp.log(summed)


def head_products(left_side, right_side, form):
    return jnp.einsum(form, left_side, right_side, preferred_element_type=jnp.float32)


def body(queries, keys, values, segments, w_out, cotangent):
    query_matrix = queries[0]
    key_rows = keys[0]
    value_rows = values[0]
    segment_row = segments[0]
    cot_rows = cotangent[0]
    local_rows = query_matrix.shape[0]
    feature_count = query_matrix.shape[1]
    head_count = feature_count // HEAD_DIM
    causal_span = HOPS * local_rows
    span_length = causal_span + local_rows
    score_scale = HEAD_DIM ** (-0.5)
    offset = lax.axis_index("cp") * local_rows
    stacked = jnp.stack([key_rows, value_rows])
    earlier = []
    moving = stacked
    for position_gap in range(HOPS):
        moving = from_behind(moving, "cp", 1)
        earlier = [moving] + earlier
    gathered = jnp.concatenate(earlier + [stacked], axis=1)
    key_heads = gathered[0].reshape(span_length, head_count, HEAD_DIM)
    value_heads = gathered[1].reshape(span_length, head_count, HEAD_DIM)
    query_heads = query_matrix.reshape(local_rows, head_count, HEAD_DIM)
    segment_padded = jnp.concatenate([-jnp.ones((causal_span,), jnp.int32), segment_row], axis=0)
    query_segs = lax.dynamic_slice_in_dim(segment_row, offset, local_rows, 0)
    key_segs = lax.dynamic_slice_in_dim(segment_padded, offset, span_length, 0)
    query_pos = offset + jnp.arange(local_rows, dtype=jnp.int32)
    key_pos = offset - causal_span + jnp.arange(span_length, dtype=jnp.int32)
    visible = (
        (query_segs[:, None] == key_segs[None, :])
        & (key_pos[None, :] <= query_pos[:, None])
        & (key_pos[None, :] >= 0)
    )
    grad_flat = lax.dot_general(
        cot_rows, w_out, (((1,), (1,)), ((), ())), preferred_element_type=jnp.float32
    )
    grad_heads = grad_flat.astype(jnp.bfloat16).reshape(local_rows, head_count, HEAD_DIM)
    query_parts = []
    attended_parts = []
    key_parts = []
    value_parts = []
    for head_index in range(head_count):
        head_slice = slice(head_index, head_index + 1)
        head_query = query_heads[:, head_slice]
        head_keys = key_heads[:, head_slice]
        head_values = value_heads[:, head_slice]
        head_grads = grad_heads[:, head_slice]
        raw_scores = head_products(head_query, head_keys, "qhd,khd->hqk")
        d_probs = head_products(head_grads, head_values, "qhd,khd->hqk")
        scores = jnp.where(visible[None], raw_scores * score_scale, NEGATIVE)
        weights = jnp.exp(scores - log_total(scores))
        rounded_probs = weights.astype(jnp.bfloat16)
        head_attended = head_products(rounded_probs, head_values, "hqk,khd->qhd").astype(
            jnp.bfloat16
        )
        row_delta = head_products(head_grads, head_attended, "qhd,qhd->hq")[..., None]
        d_scores = (weights * (d_probs - row_delta)).astype(jnp.bfloat16)
        query_parts.append(head_products(d_scores, head_keys, "hqk,khd->qhd") * score_scale)
        key_parts.append(head_products(d_scores, head_query, "hqk,qhd->khd") * score_scale)
        value_parts.append(head_products(rounded_probs, head_grads, "hqk,qhd->khd"))
        attended_parts.append(head_attended)
    attention_output = jnp.concatenate(attended_parts, axis=1)
    query_grad = jnp.concatenate(query_parts, axis=1).reshape(local_rows, feature_count)
    key_terms = jnp.concatenate(key_parts, axis=1).reshape(span_length, feature_count)
    value_terms = jnp.concatenate(value_parts, axis=1).reshape(span_length, feature_count)
    gradient_pieces = jnp.stack([key_terms, value_terms])
    partial_terms = [
        gradient_pieces[:, piece_index * local_rows : (piece_index + 1) * local_rows]
        for piece_index in range(1, HOPS)
    ]
    partial_terms = partial_terms + [gradient_pieces[:, causal_span:]]
    returned = gradient_pieces[:, :local_rows]
    for partial_term in partial_terms:
        returned = from_behind(returned, "cp", -1) + partial_term
    key_grad = returned[0]
    value_grad = returned[1]
    partial_weight = lax.dot_general(
        attention_output.reshape(local_rows, feature_count),
        cot_rows,
        (((0,), (0,)), ((), ())),
        preferred_element_type=jnp.float32,
    )
    summed = lax.psum_scatter(partial_weight, "cp", scatter_dimension=0, tiled=True)
    summed = lax.psum_scatter(summed, "dp", scatter_dimension=1, tiled=True)
    token_total = local_rows * lax.axis_size("cp") * lax.axis_size("dp")
    weight_grad = summed / math.sqrt(token_total)
    return (query_grad[None], key_grad[None], value_grad[None], weight_grad)


def solution(mesh):
    in_specs = (
        P("dp", "cp", None),
        P("dp", "cp", None),
        P("dp", "cp", None),
        P("dp", None),
        P(),
        P("dp", "cp", None),
    )
    out_specs = (P("dp", "cp", None), P("dp", "cp", None), P("dp", "cp", None), P("cp", "dp"))
    return jax.shard_map(body, mesh=mesh, in_specs=in_specs, out_specs=out_specs, check_vma=False)
```

profile of v0, /device:TPU:6, one launch (start us, length us, event | category | flops | bytes accessed | tf_op | source)
XLA Modules:
  0.0 419.3 jit_solution(12225528295627449322)
XLA Ops:
  7.2 1.1 copy.36
  9.4 4.2 %collective-permute-start = (bf16[2,128,512]{1,2,0:T(8,128)(2,1)S(1)}, bf16[2,128,512]{1,2,0:T(8,128)(2,1)S(1)}, u32[]{:S(2)}, u32[]{:S(2)}) collective-permute-start(bf16[2,128,512]{1,2,0:T(8,128)(2,1)S(1)} %pad_maximum_fusion.3), channel_id=1, source_target_pairs={{0,8},{8,16},{16,24},{24,32},{32,40},{40,48},{48,56},{56,64},{64,7... | collective-permute-start | bytes 786440 | tf_op jit(solution)/shard_map/ppermute | solution.py:18
  13.6 1.4 convolution_convert_fusion
  15.4 4.0 collective-permute-done
  19.4 6.3 %collective-permute-start.1 = (bf16[2,128,512]{1,2,0:T(8,128)(2,1)S(1)}, bf16[2,128,512]{1,2,0:T(8,128)(2,1)S(1)}, u32[]{:S(2)}, u32[]{:S(2)}) collective-permute-start(bf16[2,128,512]{1,2,0:T(8,128)(2,1)S(1)} %collective-permute-done), channel_id=1, source_target_pairs={{0,8},{8,16},{16,24},{24,32},{32,40},{40,48},{48,56},{56,64},{64,7... | collective-permute-start | bytes 786440 | tf_op jit(solution)/shard_map/ppermute | solution.py:18
  25.7 4.6 %collective-permute-done.1 = bf16[2,128,512]{1,2,0:T(8,128)(2,1)S(1)} collective-permute-done((bf16[2,128,512]{1,2,0:T(8,128)(2,1)S(1)}, bf16[2,128,512]{1,2,0:T(8,128)(2,1)S(1)}, u32[]{:S(2)}, u32[]{:S(2)}) %collective-permute-start.1) | collective-permute-done | bytes 262176 | tf_op jit(solution)/shard_map/ppermute | solution.py:18
  30.3 6.5 %collective-permute-start.2 = (bf16[2,128,512]{1,2,0:T(8,128)(2,1)S(1)}, bf16[2,128,512]{1,2,0:T(8,128)(2,1)S(1)}, u32[]{:S(2)}, u32[]{:S(2)}) collective-permute-start(bf16[2,128,512]{1,2,0:T(8,128)(2,1)S(1)} %collective-permute-done.1), channel_id=1, source_target_pairs={{0,8},{8,16},{16,24},{24,32},{32,40},{40,48},{48,56},{56,64},{64,7... | collective-permute-start | bytes 786440 | tf_op jit(solution)/shard_map/ppermute | solution.py:18
  39.4 1.3 collective-permute-done.2
  44.3 1.8 fusion.30
  49.0 1.2 convolution_bitcast_fusion
  50.2 1.2 convolution_bitcast_fusion.1
  51.4 1.2 convolution_bitcast_fusion.2
  52.6 1.0 convolution_bitcast_fusion.3
  53.9 1.9 collective-permute-start.3
  55.8 13.5 %collective-permute-done.3 = f32[2,128,512]{1,2,0:T(8,128)S(1)} collective-permute-done((f32[2,128,512]{1,2,0:T(8,128)S(1)}, f32[2,128,512]{1,2,0:T(8,128)S(1)}, u32[]{:S(2)}, u32[]{:S(2)}) %collective-permute-start.3) | collective-permute-done | bytes 524320 | tf_op jit(solution)/shard_map/ppermute | solution.py:18
  69.5 2.1 collective-permute-start.4
  71.5 13.4 %collective-permute-done.4 = f32[2,128,512]{1,2,0:T(8,128)S(1)} collective-permute-done((f32[2,128,512]{1,2,0:T(8,128)S(1)}, f32[2,128,512]{1,2,0:T(8,128)S(1)}, u32[]{:S(2)}, u32[]{:S(2)}) %collective-permute-start.4) | collective-permute-done | bytes 524320 | tf_op jit(solution)/shard_map/ppermute | solution.py:18
  85.8 1.9 collective-permute-start.5
  89.4 10.9 %collective-permute-done.5 = f32[2,128,512]{1,2,0:T(8,128)} collective-permute-done((f32[2,128,512]{1,2,0:T(8,128)}, f32[2,128,512]{1,2,0:T(8,128)}, u32[]{:S(2)}, u32[]{:S(2)}) %collective-permute-start.5) | collective-permute-done | bytes 524320 | tf_op jit(solution)/shard_map/ppermute | solution.py:18
  100.3 1.9 fusion.29
  102.3 263.0 %reduce-scatter.3.cloned.1.call-done = f32[8,1024]{1,0:T(8,128)} async-done(((f32[512,1024]{1,0:T(8,128)}), f32[8,1024]{1,0:T(8,128)}) %reduce-scatter.3.cloned.1.call-update) | async-done | bytes 32784 | tf_op jit(solution)/shard_map/reduce_scatter | solution.py:113
  365.2 1.1 fusion.50
  368.0 43.2 %reduce-scatter.5.cloned.1.call-done = f32[8,128]{1,0:T(8,128)} async-done(((f32[8,1024]{1,0:T(8,128)}), f32[8,128]{1,0:T(8,128)}) %reduce-scatter.5.cloned.1.call-update) | async-done | bytes 4112 | tf_op jit(solution)/shard_map/reduce_scatter | solution.py:114
  411.2 1.3 broadcast_multiply_fusion
  (116 shorter events, 14.5 us)
Async XLA Ops:
  7.2 6.5 %copy-start = (bf16[512,1024]{1,0:T(8,128)(2,1)S(1)}, bf16[512,1024]{1,0:T(8,128)(2,1)}, u32[]{:S(2)}) copy-start(bf16[512,1024]{1,0:T(8,128)(2,1)} %param.10) | copy-start | bytes 3145732
  7.2 29.7 %copy-start.26 = (bf16[1,128,512]{2,1,0:T(8,128)(2,1)S(1)}, bf16[1,128,512]{2,1,0:T(8,128)(2,1)}, u32[]{:S(2)}) copy-start(bf16[1,128,512]{2,1,0:T(8,128)(2,1)} %param.6) | copy-start | bytes 393220
  7.2 358.0 %reduce-scatter.3.cloned.1.call-start = ((), (), s32[]{:S(2)}) async-start(), calls=%async_computation.2 | async-start | bytes 2129920 | tf_op jit(solution)/shard_map/reduce_scatter | solution.py:113
  9.4 29.9 %copy-start.27 = (s32[1,8192]{1,0:T(1,128)S(1)}, s32[1,8192]{1,0:T(1,128)}, u32[]{:S(2)}) copy-start(s32[1,8192]{1,0:T(1,128)} %param.9) | copy-start | bytes 98308
  9.4 9.9 %collective-permute-start = (bf16[2,128,512]{1,2,0:T(8,128)(2,1)S(1)}, bf16[2,128,512]{1,2,0:T(8,128)(2,1)S(1)}, u32[]{:S(2)}, u32[]{:S(2)}) collective-permute-start(bf16[2,128,512]{1,2,0:T(8,128)(2,1)S(1)} %pad_maximum_fusion.3), channel_id=1, source_target_pairs={{0,8},{8,16},{16,24},{24,32},{32,40},{40,48},{48,56},{56,64},{64,7... | collective-permute-start | bytes 786440 | tf_op jit(solution)/shard_map/ppermute | solution.py:18
  15.3 25.4 %copy-start.13 = (bf16[128,1,128]{2,1,0:T(2,128)(2,1)}, bf16[128,1,128]{2,1,0:T(2,128)(2,1)S(1)}, u32[]{:S(2)}) copy-start(bf16[128,1,128]{2,1,0:T(2,128)(2,1)S(1)} %get-tuple-element.20) | copy-start | bytes 98308
  15.3 25.4 %copy-start.15 = (bf16[128,1,128]{2,1,0:T(2,128)(2,1)}, bf16[128,1,128]{2,1,0:T(2,128)(2,1)S(1)}, u32[]{:S(2)}) copy-start(bf16[128,1,128]{2,1,0:T(2,128)(2,1)S(1)} %get-tuple-element.22) | copy-start | bytes 98308
  15.3 25.6 %copy-start.17 = (bf16[128,1,128]{2,1,0:T(2,128)(2,1)}, bf16[128,1,128]{2,1,0:T(2,128)(2,1)S(1)}, u32[]{:S(2)}) copy-start(bf16[128,1,128]{2,1,0:T(2,128)(2,1)S(1)} %get-tuple-element.21) | copy-start | bytes 98308
  15.4 25.6 %copy-start.19 = (bf16[128,1,128]{2,1,0:T(2,128)(2,1)}, bf16[128,1,128]{2,1,0:T(2,128)(2,1)S(1)}, u32[]{:S(2)}) copy-start(bf16[128,1,128]{2,1,0:T(2,128)(2,1)S(1)} %get-tuple-element.23) | copy-start | bytes 98308
  19.4 11.0 %collective-permute-start.1 = (bf16[2,128,512]{1,2,0:T(8,128)(2,1)S(1)}, bf16[2,128,512]{1,2,0:T(8,128)(2,1)S(1)}, u32[]{:S(2)}, u32[]{:S(2)}) collective-permute-start(bf16[2,128,512]{1,2,0:T(8,128)(2,1)S(1)} %collective-permute-done), channel_id=1, source_target_pairs={{0,8},{8,16},{16,24},{24,32},{32,40},{40,48},{48,56},{56,64},{64,7... | collective-permute-start | bytes 786440 | tf_op jit(solution)/shard_map/ppermute | solution.py:18
  30.3 10.4 %collective-permute-start.2 = (bf16[2,128,512]{1,2,0:T(8,128)(2,1)S(1)}, bf16[2,128,512]{1,2,0:T(8,128)(2,1)S(1)}, u32[]{:S(2)}, u32[]{:S(2)}) collective-permute-start(bf16[2,128,512]{1,2,0:T(8,128)(2,1)S(1)} %collective-permute-done.1), channel_id=1, source_target_pairs={{0,8},{8,16},{16,24},{24,32},{32,40},{40,48},{48,56},{56,64},{64,7... | collective-permute-start | bytes 786440 | tf_op jit(solution)/shard_map/ppermute | solution.py:18
  37.0 5.0 %copy-start.21 = (bf16[1,128,512]{1,2,0:T(8,128)(2,1)}, bf16[1,128,512]{1,2,0:T(8,128)(2,1)S(1)}, u32[]{:S(2)}) copy-start(bf16[1,128,512]{1,2,0:T(8,128)(2,1)S(1)} %copy.39) | copy-start | bytes 393220
  41.3 5.8 %copy-start.3 = (f32[128,512]{0,1:T(8,128)}, f32[128,512]{0,1:T(8,128)S(1)}, u32[]{:S(2)}) copy-start(f32[128,512]{0,1:T(8,128)S(1)} %get-tuple-element.25) | copy-start | bytes 786436
  41.7 5.9 %copy-start.2 = (f32[128,512]{0,1:T(8,128)}, f32[128,512]{0,1:T(8,128)S(1)}, u32[]{:S(2)}) copy-start(f32[128,512]{0,1:T(8,128)S(1)} %get-tuple-element.29) | copy-start | bytes 786436
  42.0 6.6 %copy-start.1 = (f32[128,512]{0,1:T(8,128)}, f32[128,512]{0,1:T(8,128)S(1)}, u32[]{:S(2)}) copy-start(f32[128,512]{0,1:T(8,128)S(1)} %get-tuple-element.33) | copy-start | bytes 786436
  43.5 2.7 copy-start.6
  46.0 365.1 %reduce-scatter.5.cloned.1.call-start = ((), (), s32[]{:S(2)}) async-start(), calls=%async_computation.3 | async-start | bytes 36864 | tf_op jit(solution)/shard_map/reduce_scatter | solution.py:114
  53.9 15.5 %collective-permute-start.3 = (f32[2,128,512]{1,2,0:T(8,128)S(1)}, f32[2,128,512]{1,2,0:T(8,128)S(1)}, u32[]{:S(2)}, u32[]{:S(2)}) collective-permute-start(f32[2,128,512]{1,2,0:T(8,128)S(1)} %fusion.26), channel_id=1, source_target_pairs={{8,0},{16,8},{24,16},{32,24},{40,32},{48,40},{56,48},{64,56},{72,6... | collective-permute-start | bytes 1572872 | tf_op jit(solution)/shard_map/ppermute | solution.py:18
  69.4 18.3 %copy-start.5 = (bf16[1,512,512]{1,2,0:T(8,128)(2,1)S(1)}, bf16[1,512,512]{1,2,0:T(8,128)(2,1)}, u32[]{:S(2)}) copy-start(bf16[1,512,512]{1,2,0:T(8,128)(2,1)} %copy-done.4) | copy-start | bytes 1572868
  69.4 18.5 %copy-start.7 = (bf16[128,512]{0,1:T(8,128)(2,1)S(1)}, bf16[128,512]{0,1:T(8,128)(2,1)}, u32[]{:S(2)}) copy-start(bf16[128,512]{0,1:T(8,128)(2,1)} %copy-done.6) | copy-start | bytes 393220
  69.5 18.7 %copy-start.9 = (bf16[128,512]{0,1:T(8,128)(2,1)S(1)}, bf16[128,512]{0,1:T(8,128)(2,1)}, u32[]{:S(2)}) copy-start(bf16[128,512]{0,1:T(8,128)(2,1)} %copy-done.8) | copy-start | bytes 393220
  69.5 18.9 %copy-start.11 = (bf16[128,512]{0,1:T(8,128)(2,1)S(1)}, bf16[128,512]{0,1:T(8,128)(2,1)}, u32[]{:S(2)}) copy-start(bf16[128,512]{0,1:T(8,128)(2,1)} %copy-done.10) | copy-start | bytes 393220
  69.5 15.4 %collective-permute-start.4 = (f32[2,128,512]{1,2,0:T(8,128)S(1)}, f32[2,128,512]{1,2,0:T(8,128)S(1)}, u32[]{:S(2)}, u32[]{:S(2)}) collective-permute-start(f32[2,128,512]{1,2,0:T(8,128)S(1)} %fusion.28), channel_id=1, source_target_pairs={{8,0},{16,8},{24,16},{32,24},{40,32},{48,40},{56,48},{64,56},{72,6... | collective-permute-start | bytes 1572872 | tf_op jit(solution)/shard_map/ppermute | solution.py:18
  85.8 14.5 %collective-permute-start.5 = (f32[2,128,512]{1,2,0:T(8,128)}, f32[2,128,512]{1,2,0:T(8,128)}, u32[]{:S(2)}, u32[]{:S(2)}) collective-permute-start(f32[2,128,512]{1,2,0:T(8,128)} %fusion.25), channel_id=1, source_target_pairs={{8,0},{16,8},{24,16},{32,24},{40,32},{48,40},{56,48},{64,56},{72,6... | collective-permute-start | bytes 1572872 | tf_op jit(solution)/shard_map/ppermute | solution.py:18
  (12 other events, 18.7 us)
Sparse Core Ops, SparseCore 0:
  46.2 319.0 reduce-scatter.2
  368.2 42.8 reduce-scatter.4
where the time goes:
time: 420 us; the launch traced here: 419 us
  waiting for transfers between devices  354 us (84%)
  starting transfers between devices  22.9 us (5%)
  between operations  14.8 us (4%)
  matrix products  12.4 us (3%)
  local copies, waits for them, and re-layouts  10.1 us (2%)
  other arithmetic  5.15 us (1%)
    reduce_scatter x1, waiting for transfers between devices, body(): lax.psum_scatter(partial_weight, 'cp', scatter_dimension=0, tiled=True)  263 us
    ppermute x6, waiting for transfers between devices, from_behind(): lax.ppermute(value, axis, [(source, source + steps) for source in range(f...  47.8 us
    reduce_scatter x1, waiting for transfers between devices, body(): summed = lax.psum_scatter(summed, 'dp', scatter_dimension=1, tiled=True)  43.2 us
    ppermute x6, starting transfers between devices, from_behind(): lax.ppermute(value, axis, [(source, source + steps) for source in range(f...  22.9 us
    dot_general x24, matrix products, head_products(): jnp.einsum(form, left_side, right_side, preferred_element_type=jnp.float32)  9.22 us
  transfers between devices with their start and end apart: 8, of which 8 were waited for; matrix products, arithmetic and copies ran while one was open for 4% of the time, Pallas kernels for 0%

commit v1 on v0

v1 whole, which is shorter than its diff:
```python
import math

import jax
import jax.numpy as jnp
from jax import lax
from jax.experimental import pallas as pl
from jax.experimental.pallas import tpu as pltpu
from jax.sharding import PartitionSpec as P

HEAD_DIM = 128
ROWS = 128
MESH = pl.DeviceIdType.MESH
NEGATIVE = -1e30
F32 = jnp.float32
BF16 = jnp.bfloat16

XS = 4
PLANES = 16
PEERS = 36


def dot(left, right, left_dim, right_dim):
    return lax.dot_general(
        left, right, (((left_dim,), (right_dim,)), ((), ())), preferred_element_type=F32
    )


def kernel(
    q_hbm, k_hbm, v_hbm, seg_hbm, w_hbm, cot_hbm,
    dq_hbm, dk_hbm, dv_hbm, wg_hbm,
    kvq, seg, w_out, cot, cot_other, cots, pack_kv, pack_q, pack_do,
    pass_kv, pass_q, pass_do, own_kv, own_q, own_do, prv, outp, outn, home, nxt,
    weights_of, dk_acc, dv_acc, att,
    ya_parts, ya_got, zb_parts, zb_got, a_sum, b_sum, fin_got, results, wg_result,
    load_sem, store_sem,
    kv_send, kv_recv, q_send, q_recv, do_send, do_recv, prv_send, prv_recv,
    swap_send, swap_recv, cot_send, cot_recv, att_send, att_recv,
    home_send, home_recv, nxt_send, nxt_recv,
    ya_send, ya_recv, zb_send, zb_recv, fin_send, fin_recv, ready,
):
    cp = lax.axis_index("cp")
    dp = lax.axis_index("dp")
    x = lax.rem(cp, XS)
    plane = lax.div(cp, XS)
    z = lax.rem(plane, 8)
    y_lo = lax.div(plane, 8)
    core = lax.rem(dp, 2)
    other = dp + 1 - 2 * core
    y = lax.div(dp, 2) * 2 + y_lo
    plane_next = lax.rem(plane + 1, PLANES)
    plane_before = lax.rem(plane + PLANES - 1, PLANES)

    beside = x + 1 - 2 * lax.rem(x, 2)
    across = 3 - x
    opposite = lax.rem(x + 2, XS)
    x_high, z_high = lax.div(x, 2), lax.div(z, 4)
    side = (1 - z_high) * (1 - x_high) + z_high * x_high
    to_plane = x_high * 8 + lax.rem(x, 2) * 4
    owners = [((to_plane + group) * 4 + 2 * (1 - y_lo), dp) for group in range(4)]
    owners += [
        ((to_plane + group) * 4 + 2 * (1 - side) + 1, lax.rem(z, 4) * 2 + core)
        for group in range(4)
    ]
    head_from = 2 * y_lo + z_high
    z_from = lax.div(dp, 2) + 4 * ((1 - x_high) * y_lo + x_high * (1 - y_lo))
    odd_x = lax.rem(x, 2)
    summers = []
    for k in range(8):
        over_z = ((1 - x_high) * 8 + k) * 4 + head_from
        over_y = (k % 2 * 8 + z_from) * 4 + head_from
        summers.append(
            (over_z + odd_x * (over_y - over_z), dp + odd_x * (k // 2 * 2 + core - dp))
        )

    def along_x(step):
        return plane * XS + lax.rem(x + step, XS)

    def along_y(step):
        there = lax.rem(y + step, 8)
        return (lax.rem(there, 2) * 32 + z * 4 + x, lax.div(there, 2) * 2 + core)

    def along_z(step):
        return ((y_lo * 8 + lax.rem(z + step, 8)) * 4 + x, dp)

    def remote(source, target, send_sem, recv_sem, device):
        return pltpu.make_async_remote_copy(
            src_ref=source,
            dst_ref=target,
            send_sem=send_sem,
            recv_sem=recv_sem,
            device_id=device,
            device_id_type=MESH,
        )

    loads = [
        pltpu.make_async_copy(k_hbm, kvq.at[0], load_sem.at[0]),
        pltpu.make_async_copy(v_hbm, kvq.at[1], load_sem.at[1]),
        pltpu.make_async_copy(q_hbm, kvq.at[2], load_sem.at[2]),
        pltpu.make_async_copy(cot_hbm, cot, load_sem.at[3]),
        pltpu.make_async_copy(w_hbm, w_out, load_sem.at[4]),
        pltpu.make_async_copy(seg_hbm, seg, load_sem.at[5]),
    ]
    for load in loads:
        load.start()

    barrier = pltpu.get_barrier_semaphore()
    peers = [(along_x(step), dp) for step in range(1, XS)]
    peers += [(cp, other)] + owners + summers
    peers += [(plane_next * XS + x, dp), (plane_before * XS + x, dp)]
    peers += [along_y(step) for step in range(1, 8)]
    peers += [along_z(step) for step in range(1, 8)]
    for peer in peers:
        pl.semaphore_signal(barrier, inc=1, device_id=peer, device_id_type=MESH)

    for load in loads[:3]:
        load.wait()
    for head in range(XS):
        at = slice(head * HEAD_DIM, (head + 1) * HEAD_DIM)
        pack_kv[head, 0] = kvq[0, :, at]
        pack_kv[head, 1] = kvq[1, :, at]
        pack_q[head] = kvq[2, :, at]

    pl.semaphore_wait(barrier, PEERS)

    ring = {0: beside, 1: across, 2: opposite}

    def at_x(there):
        return (plane * XS + there, dp)

    def to_ring(pack, passing, own, send_sem, recv_sem):
        direct = [
            remote(pack.at[ring[k]], own.at[x], send_sem.at[k], recv_sem.at[k], at_x(ring[k]))
            for k in range(2)
        ]
        first = remote(pack.at[opposite], passing, send_sem.at[2], recv_sem.at[2], at_x(beside))
        second = remote(passing, own.at[beside], send_sem.at[3], recv_sem.at[3], at_x(across))
        return direct + [first, second]

    kv_copies = to_ring(pack_kv, pass_kv, own_kv, kv_send, kv_recv)
    q_copies = to_ring(pack_q, pass_q, own_q, q_send, q_recv)
    do_copies = to_ring(pack_do, pass_do, own_do, do_send, do_recv)
    for copies in (kv_copies, q_copies):
        for k in (2, 0, 1):
            copies[k].start()
    own_kv[x] = pack_kv[x]
    own_q[x] = pack_q[x]

    def prv_copy(origin):
        return remote(
            own_kv.at[origin],
            prv.at[origin - 1],
            prv_send.at[origin - 1],
            prv_recv.at[origin - 1],
            (plane_next * XS + x, dp),
        )

    def pass_on(origin):
        @pl.when(origin > 0)
        def _():
            prv_copy(origin).start()

    pass_on(x)

    loads[3].wait()
    for pair in range(4):
        at = slice(pair * 128, (pair + 1) * 128)
        even = cot[:, pair * 256 : pair * 256 + 128]
        odd = cot[:, pair * 256 + 128 : (pair + 1) * 256]
        cots[x, 0, :, at] = jnp.where(core == 0, even, odd)
        cot_other[:, at] = jnp.where(core == 0, odd, even)
    swap = remote(cot_other, cots.at[x, 1], swap_send, swap_recv, (cp, other))
    swap.start()

    for load in loads[4:]:
        load.wait()
    grads = dot(cot[...], w_out[...], 1, 1).astype(BF16)
    for head in range(XS):
        pack_do[head] = grads[:, head * HEAD_DIM : (head + 1) * HEAD_DIM]
    own_do[x] = pack_do[x]

    for copies in (kv_copies, q_copies):
        copies[2].wait_recv()
        copies[3].start()

    def cot_copy(part, kind, origin, target):
        return remote(
            cots.at[origin, part],
            cots.at[origin, part],
            cot_send.at[part, kind],
            cot_recv.at[part, kind],
            at_x(target),
        )

    cot_copies = [
        [cot_copy(part, 0, x, beside), cot_copy(part, 1, x, across)] for part in range(2)
    ]
    cot_copies[0].append(cot_copy(0, 2, beside, across))
    cot_copies[1].append(cot_copy(1, 2, across, beside))
    for k in range(2):
        cot_copies[0][k].start()
    for k in (2, 0, 1):
        do_copies[k].start()
    swap.wait_recv()
    for k in range(2):
        cot_copies[1][k].start()

    before = jnp.where(
        plane > 0,
        seg[0:1, pl.ds(pl.multiple_of(jnp.maximum(plane * 512 - 384, 0), 128), 384)],
        -1,
    )
    here = seg[0:1, pl.ds(pl.multiple_of(plane * 512, 128), 512)]
    span = jnp.concatenate([before, here], axis=1).astype(F32)
    row_at = lax.broadcasted_iota(jnp.int32, (ROWS, 4 * ROWS), 0)
    column_at = lax.broadcasted_iota(jnp.int32, (ROWS, 4 * ROWS), 1)
    causal = column_at <= row_at + 3 * ROWS

    for k, copy in zip(range(3), (kv_copies[0], kv_copies[1], kv_copies[3])):
        copy.wait_recv()
        pass_on(ring[k])
    for k in (0, 1, 3):
        q_copies[k].wait_recv()

    scale = HEAD_DIM ** (-0.5)

    def window(block, kind):
        slots = [
            prv[index, kind] if index < 3 else own_kv[index - 3, kind]
            for index in range(block, block + 4)
        ]
        return jnp.concatenate(slots, axis=0)

    def att_copy(block):
        return remote(
            att.at[0, block], att.at[1, block], att_send.at[block], att_recv.at[block], (cp, other)
        )

    for block in (3, 2, 1, 0):
        if block < 3:
            prv_copy(block + 1).wait_recv()
        query_segs = jnp.broadcast_to(
            span[:, (3 + block) * ROWS : (4 + block) * ROWS], (ROWS, ROWS)
        ).T
        query_segs = jnp.concatenate([query_segs] * 4, axis=1)
        visible = (span[:, block * ROWS : (block + 4) * ROWS] == query_segs) & causal
        raw = dot(own_q[block], window(block, 0), 1, 1) * scale
        scores = jnp.where(visible, raw, NEGATIVE)
        highest = jnp.max(scores, axis=1, keepdims=True)
        raised = jnp.exp(scores - highest)
        weights = raised * (1.0 / jnp.sum(raised, axis=1, keepdims=True))
        weights_of[block] = weights
        att[0, block] = dot(weights.astype(BF16), window(block, 1), 1, 0).astype(BF16)
        att_copy(block).start()
        if block == 3:
            do_copies[2].wait_recv()
            do_copies[3].start()

    cot_copies[0][0].wait_recv()
    cot_copies[0][2].start()
    cot_copies[1][1].wait_recv()
    cot_copies[1][2].start()

    def home_copy(there):
        return remote(
            outp.at[there],
            home.at[x],
            home_send.at[there],
            home_recv.at[x],
            (plane * XS + there, dp),
        )

    def nxt_copy(index):
        return remote(
            outn.at[index],
            nxt.at[index],
            nxt_send.at[index],
            nxt_recv.at[index],
            (plane_before * XS + x, dp),
        )

    def backward(block):
        keys = window(block, 0)
        values = window(block, 1)
        query = own_q[block]
        grad = own_do[block]
        weights = weights_of[block]
        probs = weights.astype(BF16)
        attended = att[0, block].astype(F32)
        delta = jnp.sum(grad.astype(F32) * attended, axis=1, keepdims=True)
        d_scores = (weights * (dot(grad, values, 1, 1) - delta)).astype(BF16)
        outp[block, 0] = (dot(d_scores, keys, 1, 0) * scale).astype(BF16)
        key_terms = dot(d_scores, query, 0, 0) * scale
        value_terms = dot(probs, grad, 0, 0)
        for part in range(4):
            index = block + part
            rows = slice(part * ROWS, (part + 1) * ROWS)
            if block == max(index - 3, 0):
                dk_acc[index] = key_terms[rows]
                dv_acc[index] = value_terms[rows]
            else:
                dk_acc[index] += key_terms[rows]
                dv_acc[index] += value_terms[rows]
        if block < 3:
            outn[block, 0] = dk_acc[block].astype(BF16)
            outn[block, 1] = dv_acc[block].astype(BF16)
            nxt_copy(block).start()

    def send_home(block):
        @pl.when(x != block)
        def _():
            home_copy(block).start()

    for k in (0, 1, 3):
        do_copies[k].wait_recv()
    for block in range(3):
        backward(block)

    cot_copies[0][1].wait_recv()
    cot_copies[1][0].wait_recv()
    for part in range(2):
        cot_copies[part][2].wait_recv()
    pl.semaphore_signal(ready, inc=1, device_id=(cp, other), device_id_type=MESH)
    for block in range(XS):
        att_copy(block).wait_recv()
    features = jnp.concatenate(
        [att[part, block] for part in range(2) for block in range(XS)], axis=0
    )
    columns = jnp.concatenate(
        [cots[block, part] for part in range(2) for block in range(XS)], axis=0
    )
    product = dot(features, columns, 0, 0)

    def exchange(at, device, parts, got, send_sem, recv_sem):
        return [
            remote(
                parts(lax.rem(at + step, 8)),
                got.at[step - 1],
                send_sem.at[step - 1],
                recv_sem.at[step - 1],
                device(step),
            )
            for step in range(1, 8)
        ]

    for pair in range(4):
        for half in range(2):
            for kind in range(2):
                first = half * 16 + kind * 8
                pieces = [
                    product[row : row + 8, pair * 128 : (pair + 1) * 128]
                    for row in range(first, 128, 32)
                ]
                part = jnp.concatenate(pieces, axis=0).astype(BF16)
                if kind == 0:
                    ya_parts[2 * pair + 1 - half] = part
                else:
                    zb_parts[pair + 4 * (x_high if half == 0 else 1 - x_high)] = part
    ya_copies = exchange(y, along_y, lambda at: ya_parts.at[at], ya_got, ya_send, ya_recv)
    zb_copies = exchange(z, along_z, lambda at: zb_parts.at[at], zb_got, zb_send, zb_recv)
    for pair in zip(ya_copies, zb_copies):
        for copy in pair:
            copy.start()

    backward(3)
    for there in range(XS):
        key_sum = dk_acc[there + 3]
        value_sum = dv_acc[there + 3]
        if there:
            nxt_copy(there - 1).wait_recv()
            key_sum += nxt[there - 1, 0].astype(F32)
            value_sum += nxt[there - 1, 1].astype(F32)
        outp[there, 1] = key_sum.astype(BF16)
        outp[there, 2] = value_sum.astype(BF16)
    pl.semaphore_wait(ready, 1)
    for there in range(XS):
        send_home(there)

    fin_copies = []
    for kind, (copies, parts, got, at, summed) in enumerate(
        ((ya_copies, ya_parts, ya_got, y, a_sum), (zb_copies, zb_parts, zb_got, z, b_sum))
    ):
        for copy in copies:
            copy.wait_recv()
        total = parts[at].astype(F32)
        for step in range(7):
            total += got[step].astype(F32)
        summed[...] = total
        came_along = (z, y)[kind]
        for group in range(4):
            copy = remote(
                summed.at[pl.ds(8 * group, 8)],
                fin_got.at[came_along],
                fin_send.at[4 * kind + group],
                fin_recv.at[came_along],
                owners[4 * kind + group],
            )
            copy.start()
            fin_copies.append(copy)

    for step in range(1, XS):
        there = lax.rem(x + step, XS)
        remote(
            outp.at[0],
            home.at[there],
            home_send.at[0],
            home_recv.at[there],
            (along_x(step), dp),
        ).wait_recv()
    home[x] = outp[x]

    for head in range(XS):
        at = slice(head * HEAD_DIM, (head + 1) * HEAD_DIM)
        results[0, :, at] = home[head, 0].astype(F32)
        results[1, :, at] = home[head, 1].astype(F32)
        results[2, :, at] = home[head, 2].astype(F32)
    stores = [
        pltpu.make_async_copy(results.at[index], target, store_sem.at[index])
        for index, target in enumerate((dq_hbm, dk_hbm, dv_hbm))
    ]
    for store in stores:
        store.start()

    for k in range(8):
        remote(
            a_sum.at[pl.ds(0, 8)], fin_got.at[k], fin_send.at[0], fin_recv.at[k], owners[0]
        ).wait_recv()
    total = fin_got[0]
    for k in range(1, 8):
        total += fin_got[k]
    wg_result[...] = total * (1.0 / math.sqrt(ROWS * 64 * 8))
    stores.append(pltpu.make_async_copy(wg_result, wg_hbm, store_sem.at[3]))
    stores[3].start()

    sent = kv_copies + q_copies + do_copies + [swap] + cot_copies[0] + cot_copies[1]
    for copy in sent + ya_copies + zb_copies + fin_copies:
        copy.wait_send()

    for origin in range(1, XS):
        prv_copy(origin).wait_send()
    for there in range(XS):
        att_copy(there).wait_send()

        @pl.when(x != there)
        def _(there=there):
            home_copy(there).wait_send()

    for index in range(3):
        nxt_copy(index).wait_send()
    for store in stores:
        store.wait()


def finish(*refs):
    held, held_wg, load_sem, store_sem = refs[8:]
    slots = [held.at[0], held.at[1], held.at[2], held_wg]
    loads, stores = (
        [
            pltpu.make_async_copy(source, target, sem.at[index])
            for index, (source, target) in enumerate(zip(sources, targets))
        ]
        for sources, targets, sem in (
            (refs[:4], slots, load_sem),
            (slots, refs[4:8], store_sem),
        )
    )
    for load in loads:
        load.start()
    for load, store in zip(loads, stores):
        load.wait()
        store.start()
    for store in stores:
        store.wait()


def body(queries, keys, values, segments, w_out, cotangent):
    results = [
        jax.ShapeDtypeStruct((ROWS, 512), F32),
        jax.ShapeDtypeStruct((ROWS, 512), F32),
        jax.ShapeDtypeStruct((ROWS, 512), F32),
        jax.ShapeDtypeStruct((8, 128), F32),
    ]
    dma = pltpu.SemaphoreType.DMA
    tile = (ROWS, HEAD_DIM)
    hbm = pl.BlockSpec(memory_space=pltpu.HBM)
    outs = pl.pallas_call(
        kernel,
        out_shape=results,
        in_specs=[hbm] * 6,
        out_specs=[hbm] * 4,
        scratch_shapes=[
            pltpu.VMEM((3, ROWS, 512), BF16),
            pltpu.VMEM((1, 8192), jnp.int32),
            pltpu.VMEM((512, 1024), BF16),
            pltpu.VMEM((ROWS, 1024), BF16),
            pltpu.VMEM((ROWS, 512), BF16),
            pltpu.VMEM((XS, 2, ROWS, 512), BF16),
            pltpu.VMEM((XS, 2) + tile, BF16),
            pltpu.VMEM((XS,) + tile, BF16),
            pltpu.VMEM((XS,) + tile, BF16),
            pltpu.VMEM((2,) + tile, BF16),
            pltpu.VMEM(tile, BF16),
            pltpu.VMEM(tile, BF16),
            pltpu.VMEM((XS, 2) + tile, BF16),
            pltpu.VMEM((XS,) + tile, BF16),
            pltpu.VMEM((XS,) + tile, BF16),
            pltpu.VMEM((3, 2) + tile, BF16),
            pltpu.VMEM((XS, 3) + tile, BF16),
            pltpu.VMEM((3, 2) + tile, BF16),
            pltpu.VMEM((XS, 3) + tile, BF16),
            pltpu.VMEM((3, 2) + tile, BF16),
            pltpu.VMEM((XS, ROWS, 4 * ROWS), F32),
            pltpu.VMEM((7,) + tile, F32),
            pltpu.VMEM((7,) + tile, F32),
            pltpu.VMEM((2, XS) + tile, BF16),
            pltpu.VMEM((8, 32, 128), BF16),
            pltpu.VMEM((7, 32, 128), BF16),
            pltpu.VMEM((8, 32, 128), BF16),
            pltpu.VMEM((7, 32, 128), BF16),
            pltpu.VMEM((32, 128), F32),
            pltpu.VMEM((32, 128), F32),
            pltpu.VMEM((8, 8, 128), F32),
            pltpu.VMEM((3, ROWS, 512), F32),
            pltpu.VMEM((8, 128), F32),
            dma((6,)), dma((4,)),
            dma((4,)), dma((4,)),
            dma((4,)), dma((4,)),
            dma((4,)), dma((4,)),
            dma((3,)), dma((3,)),
            dma, dma,
            dma((2, 3)), dma((2, 3)),
            dma((4,)), dma((4,)),
            dma((4,)), dma((4,)),
            dma((3,)), dma((3,)),
            dma((7,)), dma((7,)),
            dma((7,)), dma((7,)),
            dma((8,)), dma((8,)),
            pltpu.SemaphoreType.REGULAR,
        ],
        compiler_params=pltpu.CompilerParams(
            collective_id=0, has_side_effects=True, vmem_limit_bytes=60 * 1024 * 1024
        ),
        cost_estimate=pl.CostEstimate(
            flops=600_000_000, bytes_accessed=4_000_000, transcendentals=262_144
        ),
    )(queries[0], keys[0], values[0], segments, w_out, cotangent[0])
    query_grad, key_grad, value_grad, weight_grad = pl.pallas_call(
        finish,
        out_shape=results,
        in_specs=[hbm] * 4,
        out_specs=[hbm] * 4,
        scratch_shapes=[
            pltpu.VMEM((3, ROWS, 512), F32),
            pltpu.VMEM((8, 128), F32),
            dma((4,)),
            dma((4,)),
        ],
        compiler_params=pltpu.CompilerParams(vmem_limit_bytes=60 * 1024 * 1024),
        cost_estimate=pl.CostEstimate(flops=0, bytes_accessed=1_600_000, transcendentals=0),
    )(*outs)
    return (query_grad[None], key_grad[None], value_grad[None], weight_grad)


def solution(mesh):
    in_specs = (
        P("dp", "cp", None),
        P("dp", "cp", None),
        P("dp", "cp", None),
        P("dp", None),
        P(),
        P("dp", "cp", None),
    )
    out_specs = (P("dp", "cp", None), P("dp", "cp", None), P("dp", "cp", None), P("cp", "dp"))
    return jax.shard_map(body, mesh=mesh, in_specs=in_specs, out_specs=out_specs, check_vma=False)
```

time: 420 us -> 50.9 us (0.12)
  waiting for transfers between devices: 354 us -> 0 us
  Pallas kernels: 0 us -> 49.7 us
  starting transfers between devices: 22.9 us -> 0 us
  between operations: 14.8 us -> 0.64 us
  matrix products: 12.4 us -> 0 us
  local copies, waits for them, and re-layouts: 10.1 us -> 0 us
  other arithmetic: 5.15 us -> 0 us
    reduce_scatter x2 -> x0, waiting for transfers between devices: 306 us -> none  [the longest x1 263 us: body(): lax.psum_scatter(partial_weight, 'cp', scatter_dimension=0, tiled=True)]
    pallas_call x0 -> x2, Pallas kernels: none -> 49.7 us  [the longest x1 47.8 us: body(): pl.pallas_call(kernel, out_shape=results, in_specs=[hbm] * 6, out_specs=[...]
    ppermute x6 -> x0, waiting for transfers between devices: 47.8 us -> none  [from_behind(): lax.ppermute(value, axis, [(source, source + steps) for source in range(f...]
    ppermute x6 -> x0, starting transfers between devices: 22.9 us -> none  [from_behind(): lax.ppermute(value, axis, [(source, source + steps) for source in range(f...]
    dot_general x26 -> x0, matrix products: 12.4 us -> none  [the longest x24 9.22 us: head_products(): jnp.einsum(form, left_side, right_side, preferred_element_type=jnp.float32)]
    unnamed x66 -> x0, local copies, waits for them, and re-layouts: 8.36 us -> none
  transfers between devices with their start and end apart: 8 -> 0, of which waited for: 8 -> 0; matrix products, arithmetic and copies ran while one was open for 4% -> 0% of each run, Pallas kernels for 0% -> 0%
where the time goes in v1:
time: 50.9 us; the launch traced here: 50.3 us
  Pallas kernels  49.7 us (98%)
  between operations  0.64 us (1%)
    pallas_call x1, Pallas kernels, body(): pl.pallas_call(kernel, out_shape=results, in_specs=[hbm] * 6, out_specs=[...  47.8 us
    pallas_call x1, Pallas kernels, body(): pl.pallas_call(finish, out_shape=results, in_specs=[hbm] * 4, out_specs=[...  1.9 us

profile of v1, /device:TPU:6, one launch (start us, length us, event | category | flops | bytes accessed | tf_op | source)
XLA Modules:
  0.0 50.3 jit_solution(1685748175983477385)
XLA Ops:
  0.6 47.8 %shard_map.93 = (f32[128,512]{1,0:T(8,128)}, f32[128,512]{1,0:T(8,128)}, f32[128,512]{1,0:T(8,128)}, f32[8,128]{1,0:T(8,128)}) custom-call(bf16[128,512]{1,0:T(8,128)(2,1)} %bitcast.11, bf16[128,512]{1,0:T(8,128)(2,1)} %bitcast.12, bf16[128,512]{1,0:T(8,128)(2,1)} %bitcast.13, s32[1,8192]{1,0:T(1,128)} %seg_hbm.1, bf16[512,1024]{1,0:T(8,128)(2,1)} %w_hbm.1, ...), custom_call_target="tpu_custom_call" | custom-call | flops 600000000 | bytes 4000000 | tf_op jit(solution)/shard_map/pallas_call | solution.py:485
  48.4 1.9 %shard_map.94 = (f32[128,512]{1,0:T(8,128)}, f32[128,512]{1,0:T(8,128)}, f32[128,512]{1,0:T(8,128)}, f32[8,128]{1,0:T(8,128)}) custom-call(f32[128,512]{1,0:T(8,128)} %get-tuple-element.12.refs_0_, f32[128,512]{1,0:T(8,128)} %get-tuple-element.13.refs_1_, f32[128,512]{1,0:T(8,128)} %get-tuple-element.14.refs_2_, f32[8,128]{1,0:T(8,128)} %get-tuple-element.15.refs_3_), custom_call_target="tpu_custom_call" | custom-call | bytes 1600000 | tf_op jit(solution)/shard_map/pallas_call | solution.py:546

commit v2 on v1

--- a/solution.py
+++ b/solution.py
@@ -27,15 +27,15 @@
 
 def kernel(
     q_hbm, k_hbm, v_hbm, seg_hbm, w_hbm, cot_hbm,
-    dq_hbm, dk_hbm, dv_hbm, wg_hbm,
+    dq_out, dk_out, dv_out, wg_out,
     kvq, seg, w_out, cot, cot_other, cots, pack_kv, pack_q, pack_do,
-    pass_kv, pass_q, pass_do, own_kv, own_q, own_do, prv, outp, outn, home, nxt,
+    pass_kv, pass_q, pass_do, own_kv, own_q, own_do, prv, out_q, out_kv, outn, home_q, home_kv, nxt,
     weights_of, dk_acc, dv_acc, att,
-    ya_parts, ya_got, zb_parts, zb_got, a_sum, b_sum, fin_got, results, wg_result,
-    load_sem, store_sem,
+    ya_parts, ya_got, zb_parts, zb_got, a_sum, b_sum, fin_got,
+    load_sem,
     kv_send, kv_recv, q_send, q_recv, do_send, do_recv, prv_send, prv_recv,
     swap_send, swap_recv, cot_send, cot_recv, att_send, att_recv,
-    home_send, home_recv, nxt_send, nxt_recv,
+    dq_send, dq_recv, home_send, home_recv, nxt_send, nxt_recv,
     ya_send, ya_recv, zb_send, zb_recv, fin_send, fin_recv, ready,
 ):
     cp = lax.axis_index("cp")
@@ -230,14 +230,9 @@
         ]
         return jnp.concatenate(slots, axis=0)
 
-    def att_copy(block):
-        return remote(
-            att.at[0, block], att.at[1, block], att_send.at[block], att_recv.at[block], (cp, other)
-        )
-
-    for block in (3, 2, 1, 0):
-        if block < 3:
-            prv_copy(block + 1).wait_recv()
+    att_copy = remote(att.at[0], att.at[1], att_send, att_recv, (cp, other))
+
+    def forward(block):
         query_segs = jnp.broadcast_to(
             span[:, (3 + block) * ROWS : (4 + block) * ROWS], (ROWS, ROWS)
         ).T
@@ -250,20 +245,34 @@
         weights = raised * (1.0 / jnp.sum(raised, axis=1, keepdims=True))
         weights_of[block] = weights
         att[0, block] = dot(weights.astype(BF16), window(block, 1), 1, 0).astype(BF16)
-        att_copy(block).start()
-        if block == 3:
-            do_copies[2].wait_recv()
-            do_copies[3].start()
+
+    forward(3)
+    do_copies[2].wait_recv()
+    do_copies[3].start()
+    for origin in range(1, XS):
+        prv_copy(origin).wait_recv()
+    for block in (2, 1, 0):
+        forward(block)
+    att_copy.start()
 
     cot_copies[0][0].wait_recv()
     cot_copies[0][2].start()
     cot_copies[1][1].wait_recv()
     cot_copies[1][2].start()
 
+    def dq_copy(there):
+        return remote(
+            out_q.at[there],
+            home_q.at[x],
+            dq_send.at[there],
+            dq_recv.at[x],
+            (plane * XS + there, dp),
+        )
+
     def home_copy(there):
         return remote(
-            outp.at[there],
-            home.at[x],
+            out_kv.at[there],
+            home_kv.at[x],
             home_send.at[there],
             home_recv.at[x],
             (plane * XS + there, dp),
@@ -288,7 +297,7 @@
         attended = att[0, block].astype(F32)
         delta = jnp.sum(grad.astype(F32) * attended, axis=1, keepdims=True)
         d_scores = (weights * (dot(grad, values, 1, 1) - delta)).astype(BF16)
-        outp[block, 0] = (dot(d_scores, keys, 1, 0) * scale).astype(BF16)
+        out_q[block] = (dot(d_scores, keys, 1, 0) * scale).astype(BF16)
         key_terms = dot(d_scores, query, 0, 0) * scale
         value_terms = dot(probs, grad, 0, 0)
         for part in range(4):
@@ -303,25 +312,23 @@
         if block < 3:
             outn[block, 0] = dk_acc[block].astype(BF16)
             outn[block, 1] = dv_acc[block].astype(BF16)
-            nxt_copy(block).start()
-
-    def send_home(block):
+
+    def send_home(copy, block):
         @pl.when(x != block)
         def _():
-            home_copy(block).start()
+            copy(block).start()
 
     for k in (0, 1, 3):
         do_copies[k].wait_recv()
-    for block in range(3):
-        backward(block)
+    backward(0)
+    nxt_copy(0).start()
 
     cot_copies[0][1].wait_recv()
     cot_copies[1][0].wait_recv()
     for part in range(2):
         cot_copies[part][2].wait_recv()
     pl.semaphore_signal(ready, inc=1, device_id=(cp, other), device_id_type=MESH)
-    for block in range(XS):
-        att_copy(block).wait_recv()
+    att_copy.wait_recv()
     features = jnp.concatenate(
         [att[part, block] for part in range(2) for block in range(XS)], axis=0
     )
@@ -361,19 +368,13 @@
         for copy in pair:
             copy.start()
 
-    backward(3)
-    for there in range(XS):
-        key_sum = dk_acc[there + 3]
-        value_sum = dv_acc[there + 3]
-        if there:
-            nxt_copy(there - 1).wait_recv()
-            key_sum += nxt[there - 1, 0].astype(F32)
-            value_sum += nxt[there - 1, 1].astype(F32)
-        outp[there, 1] = key_sum.astype(BF16)
-        outp[there, 2] = value_sum.astype(BF16)
+    backward(1)
+    backward(2)
+    for block in (1, 2):
+        nxt_copy(block).start()
     pl.semaphore_wait(ready, 1)
-    for there in range(XS):
-        send_home(there)
+    for block in range(3):
+        send_home(dq_copy, block)
 
     fin_copies = []
     for kind, (copies, parts, got, at, summed) in enumerate(
@@ -397,29 +398,41 @@
             copy.start()
             fin_copies.append(copy)
 
+    backward(3)
+    send_home(dq_copy, 3)
+    for there in range(XS):
+        key_sum = dk_acc[there + 3]
+        value_sum = dv_acc[there + 3]
+        if there:
+            nxt_copy(there - 1).wait_recv()
+            key_sum += nxt[there - 1, 0].astype(F32)
+            value_sum += nxt[there - 1, 1].astype(F32)
+        out_kv[there, 0] = key_sum.astype(BF16)
+        out_kv[there, 1] = value_sum.astype(BF16)
+    for there in range(XS):
+        send_home(home_copy, there)
+
     for step in range(1, XS):
         there = lax.rem(x + step, XS)
-        remote(
-            outp.at[0],
-            home.at[there],
-            home_send.at[0],
-            home_recv.at[there],
-            (along_x(step), dp),
-        ).wait_recv()
-    home[x] = outp[x]
+        for source, target, send_sem, recv_sem in (
+            (out_q, home_q, dq_send, dq_recv),
+            (out_kv, home_kv, home_send, home_recv),
+        ):
+            remote(
+                source.at[0],
+                target.at[there],
+                send_sem.at[0],
+                recv_sem.at[there],
+                (along_x(step), dp),
+            ).wait_recv()
+    home_q[x] = out_q[x]
+    home_kv[x] = out_kv[x]
 
     for head in range(XS):
         at = slice(head * HEAD_DIM, (head + 1) * HEAD_DIM)
-        results[0, :, at] = home[head, 0].astype(F32)
-        results[1, :, at] = home[head, 1].astype(F32)
-        results[2, :, at] = home[head, 2].astype(F32)
-    stores = [
-        pltpu.make_async_copy(results.at[index], target, store_sem.at[index])
-        for index, target in enumerate((dq_hbm, dk_hbm, dv_hbm))
-    ]
-    for store in stores:
-        store.start()
-
+        dq_out[:, at] = home_q[head].astype(F32)
+        dk_out[:, at] = home_kv[head, 0].astype(F32)
+        dv_out[:, at] = home_kv[head, 1].astype(F32)
     for k in range(8):
         remote(
             a_sum.at[pl.ds(0, 8)], fin_got.at[k], fin_send.at[0], fin_recv.at[k], owners[0]
@@ -427,49 +440,34 @@
     total = fin_got[0]
     for k in range(1, 8):
         total += fin_got[k]
-    wg_result[...] = total * (1.0 / math.sqrt(ROWS * 64 * 8))
-    stores.append(pltpu.make_async_copy(wg_result, wg_hbm, store_sem.at[3]))
-    stores[3].start()
-
-    sent = kv_copies + q_copies + do_copies + [swap] + cot_copies[0] + cot_copies[1]
+    wg_out[...] = total * (1.0 / math.sqrt(ROWS * 64 * 8))
+
+    sent = kv_copies + q_copies + do_copies + [swap, att_copy] + cot_copies[0] + cot_copies[1]
     for copy in sent + ya_copies + zb_copies + fin_copies:
         copy.wait_send()
 
     for origin in range(1, XS):
         prv_copy(origin).wait_send()
     for there in range(XS):
-        att_copy(there).wait_send()
 
         @pl.when(x != there)
         def _(there=there):
+            dq_copy(there).wait_send()
             home_copy(there).wait_send()
 
     for index in range(3):
         nxt_copy(index).wait_send()
-    for store in stores:
-        store.wait()
 
 
 def finish(*refs):
-    held, held_wg, load_sem, store_sem = refs[8:]
-    slots = [held.at[0], held.at[1], held.at[2], held_wg]
-    loads, stores = (
-        [
-            pltpu.make_async_copy(source, target, sem.at[index])
-            for index, (source, target) in enumerate(zip(sources, targets))
-        ]
-        for sources, targets, sem in (
-            (refs[:4], slots, load_sem),
-            (slots, refs[4:8], store_sem),
-        )
-    )
-    for load in loads:
-        load.start()
-    for load, store in zip(loads, stores):
-        load.wait()
-        store.start()
-    for store in stores:
-        store.wait()
+    copies = [
+        pltpu.make_async_copy(refs[index], refs[4 + index], refs[8].at[index])
+        for index in range(4)
+    ]
+    for copy in copies:
+        copy.start()
+    for copy in copies:
+        copy.wait()
 
 
 def body(queries, keys, values, segments, w_out, cotangent):
@@ -482,11 +480,14 @@
     dma = pltpu.SemaphoreType.DMA
     tile = (ROWS, HEAD_DIM)
     hbm = pl.BlockSpec(memory_space=pltpu.HBM)
+    vmem = pl.BlockSpec(memory_space=pltpu.VMEM)
+    operands = [queries[0], keys[0], values[0], segments, w_out, cotangent[0]]
+    operands = [pltpu.with_memory_space_constraint(operand, pltpu.HBM) for operand in operands]
     outs = pl.pallas_call(
         kernel,
-        out_shape=results,
+        out_shape=[pltpu.VMEM(result.shape, result.dtype) for result in results],
         in_specs=[hbm] * 6,
-        out_specs=[hbm] * 4,
+        out_specs=[vmem] * 4,
         scratch_shapes=[
             pltpu.VMEM((3, ROWS, 512), BF16),
             pltpu.VMEM((1, 8192), jnp.int32),
@@ -504,9 +505,11 @@
             pltpu.VMEM((XS,) + tile, BF16),
             pltpu.VMEM((XS,) + tile, BF16),
             pltpu.VMEM((3, 2) + tile, BF16),
-            pltpu.VMEM((XS, 3) + tile, BF16),
+            pltpu.VMEM((XS,) + tile, BF16),
+            pltpu.VMEM((XS, 2) + tile, BF16),
             pltpu.VMEM((3, 2) + tile, BF16),
-            pltpu.VMEM((XS, 3) + tile, BF16),
+            pltpu.VMEM((XS,) + tile, BF16),
+            pltpu.VMEM((XS, 2) + tile, BF16),
             pltpu.VMEM((3, 2) + tile, BF16),
             pltpu.VMEM((XS, ROWS, 4 * ROWS), F32),
             pltpu.VMEM((7,) + tile, F32),
@@ -519,15 +522,14 @@
             pltpu.VMEM((32, 128), F32),
             pltpu.VMEM((32, 128), F32),
             pltpu.VMEM((8, 8, 128), F32),
-            pltpu.VMEM((3, ROWS, 512), F32),
-            pltpu.VMEM((8, 128), F32),
-            dma((6,)), dma((4,)),
+            dma((6,)),
             dma((4,)), dma((4,)),
             dma((4,)), dma((4,)),
             dma((4,)), dma((4,)),
             dma((3,)), dma((3,)),
             dma, dma,
             dma((2, 3)), dma((2, 3)),
+            dma, dma,
             dma((4,)), dma((4,)),
             dma((4,)), dma((4,)),
             dma((3,)), dma((3,)),
@@ -537,24 +539,19 @@
             pltpu.SemaphoreType.REGULAR,
         ],
         compiler_params=pltpu.CompilerParams(
-            collective_id=0, has_side_effects=True, vmem_limit_bytes=60 * 1024 * 1024
+            collective_id=0, has_side_effects=True, vmem_limit_bytes=32 * 1024 * 1024
         ),
         cost_estimate=pl.CostEstimate(
             flops=600_000_000, bytes_accessed=4_000_000, transcendentals=262_144
         ),
-    )(queries[0], keys[0], values[0], segments, w_out, cotangent[0])
+    )(*operands)
     query_grad, key_grad, value_grad, weight_grad = pl.pallas_call(
         finish,
         out_shape=results,
-        in_specs=[hbm] * 4,
+        in_specs=[vmem] * 4,
         out_specs=[hbm] * 4,
-        scratch_shapes=[
-            pltpu.VMEM((3, ROWS, 512), F32),
-            pltpu.VMEM((8, 128), F32),
-            dma((4,)),
-            dma((4,)),
-        ],
-        compiler_params=pltpu.CompilerParams(vmem_limit_bytes=60 * 1024 * 1024),
+        scratch_shapes=[dma((4,))],
+        compiler_params=pltpu.CompilerParams(vmem_limit_bytes=4 * 1024 * 1024),
         cost_estimate=pl.CostEstimate(flops=0, bytes_accessed=1_600_000, transcendentals=0),
     )(*outs)
     return (query_grad[None], key_grad[None], value_grad[None], weight_grad)

time: 50.9 us -> 49.3 us (0.969)
  Pallas kernels: 49.7 us -> 48.3 us
    pallas_call x2, Pallas kernels: 49.7 us -> 48.3 us  [the longest x1 47.4 us: body(): pl.pallas_call(kernel, out_shape=[pltpu.VMEM(result.shape, result.dtype)...]
where the time goes in v2:
time: 49.3 us; the launch traced here: 49 us
  Pallas kernels  48.3 us (98%)
  between operations  0.64 us (1%)
    pallas_call x1, Pallas kernels, body(): pl.pallas_call(kernel, out_shape=[pltpu.VMEM(result.shape, result.dtype)...  47.4 us

profile of v2, /device:TPU:6, one launch (start us, length us, event | category | flops | bytes accessed | tf_op | source)
XLA Modules:
  0.0 49.0 jit_solution(14034422503991244131)
XLA Ops:
  0.6 47.4 %shard_map.93 = (f32[128,512]{1,0:T(8,128)S(1)}, f32[128,512]{1,0:T(8,128)S(1)}, f32[128,512]{1,0:T(8,128)S(1)}, f32[8,128]{1,0:T(8,128)S(1)}) custom-call(bf16[128,512]{1,0:T(8,128)(2,1)} %bitcast.11, bf16[128,512]{1,0:T(8,128)(2,1)} %bitcast.12, bf16[128,512]{1,0:T(8,128)(2,1)} %bitcast.13, s32[1,8192]{1,0:T(1,128)} %seg_hbm.1, bf16[512,1024]{1,0:T(8,128)(2,1)} %w_hbm.1, ...), custom_call_target="tpu_custom_call" | custom-call | flops 600000000 | bytes 4000000 | tf_op jit(solution)/shard_map/pallas_call | solution.py:486
  48.0 0.9 %shard_map.94 = (f32[128,512]{1,0:T(8,128)}, f32[128,512]{1,0:T(8,128)}, f32[128,512]{1,0:T(8,128)}, f32[8,128]{1,0:T(8,128)}) custom-call(f32[128,512]{1,0:T(8,128)S(1)} %get-tuple-element.12.refs_0_, f32[128,512]{1,0:T(8,128)S(1)} %get-tuple-element.13.refs_1_, f32[128,512]{1,0:T(8,128)S(1)} %get-tuple-element.14.refs_2_, ...), custom_call_target="tpu_custom_call" | custom-call | bytes 1600000 | tf_op jit(solution)/shard_map/pallas_call | solution.py:548

commit v3 on v2

--- a/solution.py
+++ b/solution.py
@@ -251,14 +251,14 @@
     do_copies[3].start()
     for origin in range(1, XS):
         prv_copy(origin).wait_recv()
-    for block in (2, 1, 0):
-        forward(block)
-    att_copy.start()
-
+    forward(2)
     cot_copies[0][0].wait_recv()
     cot_copies[0][2].start()
+    forward(1)
     cot_copies[1][1].wait_recv()
     cot_copies[1][2].start()
+    forward(0)
+    att_copy.start()
 
     def dq_copy(there):
         return remote(

time: 49.3 us -> 49.3 us (level)
  no operation moved by 1% of the time
where the time goes in v3:
time: 49.3 us; the launch traced here: 49 us
  Pallas kernels  48.4 us (98%)
  between operations  0.64 us (1%)
    pallas_call x1, Pallas kernels, body(): pl.pallas_call(kernel, out_shape=[pltpu.VMEM(result.shape, result.dtype)...  47.5 us

profile of v3, /device:TPU:6, one launch (start us, length us, event | category | flops | bytes accessed | tf_op | source)
XLA Modules:
  0.0 49.0 jit_solution(1655893795475496692)
XLA Ops:
  0.6 47.5 %shard_map.93 = (f32[128,512]{1,0:T(8,128)S(1)}, f32[128,512]{1,0:T(8,128)S(1)}, f32[128,512]{1,0:T(8,128)S(1)}, f32[8,128]{1,0:T(8,128)S(1)}) custom-call(bf16[128,512]{1,0:T(8,128)(2,1)} %bitcast.11, bf16[128,512]{1,0:T(8,128)(2,1)} %bitcast.12, bf16[128,512]{1,0:T(8,128)(2,1)} %bitcast.13, s32[1,8192]{1,0:T(1,128)} %seg_hbm.1, bf16[512,1024]{1,0:T(8,128)(2,1)} %w_hbm.1, ...), custom_call_target="tpu_custom_call" | custom-call | flops 600000000 | bytes 4000000 | tf_op jit(solution)/shard_map/pallas_call | solution.py:486
  48.1 0.9 %shard_map.94 = (f32[128,512]{1,0:T(8,128)}, f32[128,512]{1,0:T(8,128)}, f32[128,512]{1,0:T(8,128)}, f32[8,128]{1,0:T(8,128)}) custom-call(f32[128,512]{1,0:T(8,128)S(1)} %get-tuple-element.12.refs_0_, f32[128,512]{1,0:T(8,128)S(1)} %get-tuple-element.13.refs_1_, f32[128,512]{1,0:T(8,128)S(1)} %get-tuple-element.14.refs_2_, ...), custom_call_target="tpu_custom_call" | custom-call | bytes 1600000 | tf_op jit(solution)/shard_map/pallas_call | solution.py:548

commit v4 on v2

--- a/solution.py
+++ b/solution.py
@@ -29,13 +29,15 @@
     q_hbm, k_hbm, v_hbm, seg_hbm, w_hbm, cot_hbm,
     dq_out, dk_out, dv_out, wg_out,
     kvq, seg, w_out, cot, cot_other, cots, pack_kv, pack_q, pack_do,
-    pass_kv, pass_q, pass_do, own_kv, own_q, own_do, prv, out_q, out_kv, outn, home_q, home_kv, nxt,
+    pass_kv, pass_q, pass_do, own_kv, own_q, own_do, prv, out_q, out_k, out_v, outn_k, outn_v,
+    home_q, home_k, home_v, nxt_k, nxt_v,
     weights_of, dk_acc, dv_acc, att,
     ya_parts, ya_got, zb_parts, zb_got, a_sum, b_sum, fin_got,
     load_sem,
     kv_send, kv_recv, q_send, q_recv, do_send, do_recv, prv_send, prv_recv,
     swap_send, swap_recv, cot_send, cot_recv, att_send, att_recv,
-    dq_send, dq_recv, home_send, home_recv, nxt_send, nxt_recv,
+    dq_send, dq_recv, dk_send, dk_recv, dv_send, dv_recv,
+    nk_send, nk_recv, nv_send, nv_recv,
     ya_send, ya_recv, zb_send, zb_recv, fin_send, fin_recv, ready,
 ):
     cp = lax.axis_index("cp")
@@ -260,32 +262,40 @@
     cot_copies[1][1].wait_recv()
     cot_copies[1][2].start()
 
-    def dq_copy(there):
-        return remote(
-            out_q.at[there],
-            home_q.at[x],
-            dq_send.at[there],
-            dq_recv.at[x],
-            (plane * XS + there, dp),
-        )
-
-    def home_copy(there):
-        return remote(
-            out_kv.at[there],
-            home_kv.at[x],
-            home_send.at[there],
-            home_recv.at[x],
-            (plane * XS + there, dp),
-        )
-
-    def nxt_copy(index):
-        return remote(
-            outn.at[index],
-            nxt.at[index],
-            nxt_send.at[index],
-            nxt_recv.at[index],
-            (plane_before * XS + x, dp),
-        )
+    def to_home(out, home, send_sem, recv_sem):
+        return [
+            remote(
+                out.at[there],
+                home.at[x],
+                send_sem.at[there],
+                recv_sem.at[x],
+                (plane * XS + there, dp),
+            )
+            for there in range(XS)
+        ]
+
+    dq_copies = to_home(out_q, home_q, dq_send, dq_recv)
+    dk_copies = to_home(out_k, home_k, dk_send, dk_recv)
+    dv_copies = to_home(out_v, home_v, dv_send, dv_recv)
+
+    nk_copy = remote(outn_k, nxt_k, nk_send, nk_recv, (plane_before * XS + x, dp))
+    nv_copy = remote(outn_v, nxt_v, nv_send, nv_recv, (plane_before * XS + x, dp))
+
+    def accumulate(total_ref, block, terms):
+        for part in range(4):
+            index = block + part
+            rows = slice(part * ROWS, (part + 1) * ROWS)
+            if block == max(index - 3, 0):
+                total_ref[index] = terms[rows]
+            else:
+                total_ref[index] += terms[rows]
+
+    def add_next(total_ref, nxt, out):
+        for there in range(XS):
+            total = total_ref[there + 3]
+            if there:
+                total += nxt[there - 1].astype(F32)
+            out[there] = total.astype(BF16)
 
     def backward(block):
         keys = window(block, 0)
@@ -293,35 +303,24 @@
         query = own_q[block]
         grad = own_do[block]
         weights = weights_of[block]
-        probs = weights.astype(BF16)
         attended = att[0, block].astype(F32)
         delta = jnp.sum(grad.astype(F32) * attended, axis=1, keepdims=True)
         d_scores = (weights * (dot(grad, values, 1, 1) - delta)).astype(BF16)
         out_q[block] = (dot(d_scores, keys, 1, 0) * scale).astype(BF16)
-        key_terms = dot(d_scores, query, 0, 0) * scale
-        value_terms = dot(probs, grad, 0, 0)
-        for part in range(4):
-            index = block + part
-            rows = slice(part * ROWS, (part + 1) * ROWS)
-            if block == max(index - 3, 0):
-                dk_acc[index] = key_terms[rows]
-                dv_acc[index] = value_terms[rows]
-            else:
-                dk_acc[index] += key_terms[rows]
-                dv_acc[index] += value_terms[rows]
-        if block < 3:
-            outn[block, 0] = dk_acc[block].astype(BF16)
-            outn[block, 1] = dv_acc[block].astype(BF16)
-
-    def send_home(copy, block):
+        accumulate(dk_acc, block, dot(d_scores, query, 0, 0) * scale)
+
+    def send_home(copies, block):
         @pl.when(x != block)
         def _():
-            copy(block).start()
+            copies[block].start()
 
     for k in (0, 1, 3):
         do_copies[k].wait_recv()
-    backward(0)
-    nxt_copy(0).start()
+    for block in range(XS):
+        accumulate(dv_acc, block, dot(weights_of[block].astype(BF16), own_do[block], 0, 0))
+    for index in range(3):
+        outn_v[index] = dv_acc[index].astype(BF16)
+    nv_copy.start()
 
     cot_copies[0][1].wait_recv()
     cot_copies[1][0].wait_recv()
@@ -368,13 +367,18 @@
         for copy in pair:
             copy.start()
 
-    backward(1)
-    backward(2)
-    for block in (1, 2):
-        nxt_copy(block).start()
+    for block in range(3):
+        backward(block)
+    for index in range(3):
+        outn_k[index] = dk_acc[index].astype(BF16)
+    nk_copy.start()
+    nv_copy.wait_recv()
+    add_next(dv_acc, nxt_v, out_v)
     pl.semaphore_wait(ready, 1)
     for block in range(3):
-        send_home(dq_copy, block)
+        send_home(dq_copies, block)
+    for block in range(XS):
+        send_home(dv_copies, block)
 
     fin_copies = []
     for kind, (copies, parts, got, at, summed) in enumerate(
@@ -399,24 +403,18 @@
             fin_copies.append(copy)
 
     backward(3)
-    send_home(dq_copy, 3)
+    send_home(dq_copies, 3)
+    nk_copy.wait_recv()
+    add_next(dk_acc, nxt_k, out_k)
     for there in range(XS):
-        key_sum = dk_acc[there + 3]
-        value_sum = dv_acc[there + 3]
-        if there:
-            nxt_copy(there - 1).wait_recv()
-            key_sum += nxt[there - 1, 0].astype(F32)
-            value_sum += nxt[there - 1, 1].astype(F32)
-        out_kv[there, 0] = key_sum.astype(BF16)
-        out_kv[there, 1] = value_sum.astype(BF16)
-    for there in range(XS):
-        send_home(home_copy, there)
+        send_home(dk_copies, there)
 
     for step in range(1, XS):
         there = lax.rem(x + step, XS)
         for source, target, send_sem, recv_sem in (
             (out_q, home_q, dq_send, dq_recv),
-            (out_kv, home_kv, home_send, home_recv),
+            (out_k, home_k, dk_send, dk_recv),
+            (out_v, home_v, dv_send, dv_recv),
         ):
             remote(
                 source.at[0],
@@ -426,13 +424,14 @@
                 (along_x(step), dp),
             ).wait_recv()
     home_q[x] = out_q[x]
-    home_kv[x] = out_kv[x]
+    home_k[x] = out_k[x]
+    home_v[x] = out_v[x]
 
     for head in range(XS):
         at = slice(head * HEAD_DIM, (head + 1) * HEAD_DIM)
         dq_out[:, at] = home_q[head].astype(F32)
-        dk_out[:, at] = home_kv[head, 0].astype(F32)
-        dv_out[:, at] = home_kv[head, 1].astype(F32)
+        dk_out[:, at] = home_k[head].astype(F32)
+        dv_out[:, at] = home_v[head].astype(F32)
     for k in range(8):
         remote(
             a_sum.at[pl.ds(0, 8)], fin_got.at[k], fin_send.at[0], fin_recv.at[k], owners[0]
@@ -452,11 +451,11 @@
 
         @pl.when(x != there)
         def _(there=there):
-            dq_copy(there).wait_send()
-            home_copy(there).wait_send()
-
-    for index in range(3):
-        nxt_copy(index).wait_send()
+            for copies in (dq_copies, dk_copies, dv_copies):
+                copies[there].wait_send()
+
+    nk_copy.wait_send()
+    nv_copy.wait_send()
 
 
 def finish(*refs):
@@ -506,11 +505,15 @@
             pltpu.VMEM((XS,) + tile, BF16),
             pltpu.VMEM((3, 2) + tile, BF16),
             pltpu.VMEM((XS,) + tile, BF16),
-            pltpu.VMEM((XS, 2) + tile, BF16),
-            pltpu.VMEM((3, 2) + tile, BF16),
-            pltpu.VMEM((XS,) + tile, BF16),
-            pltpu.VMEM((XS, 2) + tile, BF16),
-            pltpu.VMEM((3, 2) + tile, BF16),
+            pltpu.VMEM((XS,) + tile, BF16),
+            pltpu.VMEM((XS,) + tile, BF16),
+            pltpu.VMEM((3,) + tile, BF16),
+            pltpu.VMEM((3,) + tile, BF16),
+            pltpu.VMEM((XS,) + tile, BF16),
+            pltpu.VMEM((XS,) + tile, BF16),
+            pltpu.VMEM((XS,) + tile, BF16),
+            pltpu.VMEM((3,) + tile, BF16),
+            pltpu.VMEM((3,) + tile, BF16),
             pltpu.VMEM((XS, ROWS, 4 * ROWS), F32),
             pltpu.VMEM((7,) + tile, F32),
             pltpu.VMEM((7,) + tile, F32),
@@ -532,7 +535,9 @@
             dma, dma,
             dma((4,)), dma((4,)),
             dma((4,)), dma((4,)),
-            dma((3,)), dma((3,)),
+            dma((4,)), dma((4,)),
+            dma, dma,
+            dma, dma,
             dma((7,)), dma((7,)),
             dma((7,)), dma((7,)),
             dma((8,)), dma((8,)),

time: 49.3 us -> 49.5 us (level)
  no operation moved by 1% of the time
where the time goes in v4:
time: 49.5 us; the launch traced here: 49.1 us
  Pallas kernels  48.5 us (98%)
  between operations  0.64 us (1%)
    pallas_call x1, Pallas kernels, body(): pl.pallas_call(kernel, out_shape=[pltpu.VMEM(result.shape, result.dtype)...  47.6 us

profile of v4, /device:TPU:6, one launch (start us, length us, event | category | flops | bytes accessed | tf_op | source)
XLA Modules:
  0.0 49.1 jit_solution(1817937605447088758)
XLA Ops:
  0.6 47.6 %shard_map.93 = (f32[128,512]{1,0:T(8,128)S(1)}, f32[128,512]{1,0:T(8,128)S(1)}, f32[128,512]{1,0:T(8,128)S(1)}, f32[8,128]{1,0:T(8,128)S(1)}) custom-call(bf16[128,512]{1,0:T(8,128)(2,1)} %bitcast.11, bf16[128,512]{1,0:T(8,128)(2,1)} %bitcast.12, bf16[128,512]{1,0:T(8,128)(2,1)} %bitcast.13, s32[1,8192]{1,0:T(1,128)} %seg_hbm.1, bf16[512,1024]{1,0:T(8,128)(2,1)} %w_hbm.1, ...), custom_call_target="tpu_custom_call" | custom-call | flops 600000000 | bytes 4000000 | tf_op jit(solution)/shard_map/pallas_call | solution.py:485
  48.2 0.9 %shard_map.94 = (f32[128,512]{1,0:T(8,128)}, f32[128,512]{1,0:T(8,128)}, f32[128,512]{1,0:T(8,128)}, f32[8,128]{1,0:T(8,128)}) custom-call(f32[128,512]{1,0:T(8,128)S(1)} %get-tuple-element.12.refs_0_, f32[128,512]{1,0:T(8,128)S(1)} %get-tuple-element.13.refs_1_, f32[128,512]{1,0:T(8,128)S(1)} %get-tuple-element.14.refs_2_, ...), custom_call_target="tpu_custom_call" | custom-call | bytes 1600000 | tf_op jit(solution)/shard_map/pallas_call | solution.py:553

commit v5 on v2

--- a/solution.py
+++ b/solution.py
@@ -198,11 +198,11 @@
     cot_copies[1].append(cot_copy(1, 2, across, beside))
     for k in range(2):
         cot_copies[0][k].start()
-    for k in (2, 0, 1):
-        do_copies[k].start()
     swap.wait_recv()
     for k in range(2):
         cot_copies[1][k].start()
+    for k in (2, 0, 1):
+        do_copies[k].start()
 
     before = jnp.where(
         plane > 0,
@@ -247,13 +247,13 @@
         att[0, block] = dot(weights.astype(BF16), window(block, 1), 1, 0).astype(BF16)
 
     forward(3)
-    do_copies[2].wait_recv()
-    do_copies[3].start()
     for origin in range(1, XS):
         prv_copy(origin).wait_recv()
     for block in (2, 1, 0):
         forward(block)
     att_copy.start()
+    do_copies[2].wait_recv()
+    do_copies[3].start()
 
     cot_copies[0][0].wait_recv()
     cot_copies[0][2].start()
@@ -318,10 +318,6 @@
         def _():
             copy(block).start()
 
-    for k in (0, 1, 3):
-        do_copies[k].wait_recv()
-    backward(0)
-    nxt_copy(0).start()
 
     cot_copies[0][1].wait_recv()
     cot_copies[1][0].wait_recv()
@@ -368,6 +364,10 @@
         for copy in pair:
             copy.start()
 
+    for k in (0, 1, 3):
+        do_copies[k].wait_recv()
+    backward(0)
+    nxt_copy(0).start()
     backward(1)
     backward(2)
     for block in (1, 2):

time: 49.3 us -> 49.5 us (level)
  no operation moved by 1% of the time
where the time goes in v5:
time: 49.5 us; the launch traced here: 49.4 us
  Pallas kernels  48.7 us (98%)
  between operations  0.64 us (1%)
    pallas_call x1, Pallas kernels, body(): pl.pallas_call(kernel, out_shape=[pltpu.VMEM(result.shape, result.dtype)...  47.8 us

profile of v5, /device:TPU:6, one launch (start us, length us, event | category | flops | bytes accessed | tf_op | source)
XLA Modules:
  0.0 49.4 jit_solution(12676885778020456372)
XLA Ops:
  0.6 47.8 %shard_map.93 = (f32[128,512]{1,0:T(8,128)S(1)}, f32[128,512]{1,0:T(8,128)S(1)}, f32[128,512]{1,0:T(8,128)S(1)}, f32[8,128]{1,0:T(8,128)S(1)}) custom-call(bf16[128,512]{1,0:T(8,128)(2,1)} %bitcast.11, bf16[128,512]{1,0:T(8,128)(2,1)} %bitcast.12, bf16[128,512]{1,0:T(8,128)(2,1)} %bitcast.13, s32[1,8192]{1,0:T(1,128)} %seg_hbm.1, bf16[512,1024]{1,0:T(8,128)(2,1)} %w_hbm.1, ...), custom_call_target="tpu_custom_call" | custom-call | flops 600000000 | bytes 4000000 | tf_op jit(solution)/shard_map/pallas_call | solution.py:486
  48.5 0.9 %shard_map.94 = (f32[128,512]{1,0:T(8,128)}, f32[128,512]{1,0:T(8,128)}, f32[128,512]{1,0:T(8,128)}, f32[8,128]{1,0:T(8,128)}) custom-call(f32[128,512]{1,0:T(8,128)S(1)} %get-tuple-element.12.refs_0_, f32[128,512]{1,0:T(8,128)S(1)} %get-tuple-element.13.refs_1_, f32[128,512]{1,0:T(8,128)S(1)} %get-tuple-element.14.refs_2_, ...), custom_call_target="tpu_custom_call" | custom-call | bytes 1600000 | tf_op jit(solution)/shard_map/pallas_call | solution.py:548
